TPU v7x, 32 devices: a whole 2x2x4 slice. The times are simulated.
32 devices in a mesh: rev: 2 (over x), bin: 16 (over z, y, core).
Axes of the slice: x: 2, y: 2, z: 4, core: 2. Of those that a mesh axis runs over, the one named last changes fastest.
Arguments:
- snapshots: float32 [2, 512, 3, 6, 8, 128], P('rev', 'bin'), may hold values from -6 to 6
- phase_index: int32 [2, 512], P('rev', 'bin'), may hold values from 0 to 255, as said below
Outputs:
- stress_terms: float32 [4, 6, 256, 6, 8, 128], P(None, None, 'bin', 'rev')
- mean_velocity: float32 [3, 256, 6, 8, 128], P(None, 'bin', 'rev')
Inputs may be any that keep to these rules, and one draw needn't show every extreme that they name: `phase_index`: the rows b * 32 to (b + 1) * 32 - 1 of a revolution shard name bins b * 16 to (b + 1) * 16 - 1 only, and each of these bins at least once.
All inputs are finite; a program needn't handle non-finite values.
Results may differ from a plain program's by a relative error of at most 0.00017.
Values sent between devices are 32-bit elements; how exact they have to be, the bound alone decides.
A program may use at most 64 MiB of HBM per device.

v0:
```python
import functools

import jax
import jax.numpy as jnp
from jax import lax
from jax.experimental import pallas as pl
from jax.experimental.pallas import tpu as pltpu
from jax.sharding import PartitionSpec as P

PHASES = 256


viscosity = 0.2
stress_pairs = ((0, 0), (0, 1), (0, 2), (1, 1), (1, 2), (2, 2))


def padded_2(cells, sides, width):
    for axis, dim in sides:
        count = lax.axis_size(axis)
        head = lax.slice_in_dim(cells, 0, width, axis=dim)
        tail = lax.slice_in_dim(cells, cells.shape[dim] - width, cells.shape[dim], axis=dim)
        cells = jnp.concatenate(
            [
                lax.ppermute(tail, axis, [(i, (i + 1) % count) for i in range(count)]),
                cells,
                lax.ppermute(head, axis, [((i + 1) % count, i) for i in range(count)]),
            ],
            axis=dim,
        )
    return cells


def pair_index(first, second):
    low, high = (min(first, second), max(first, second))
    return stress_pairs.index((low, high))


def binned(frames, weights):
    vel_x, vel_y, vel_z = (frames[:, 0], frames[:, 1], frames[:, 2])
    stacked = jnp.stack(
        [
            jnp.ones_like(vel_x),
            vel_x,
            vel_y,
            vel_z,
            vel_x * vel_x,
            vel_x * vel_y,
            vel_x * vel_z,
            vel_y * vel_y,
            vel_y * vel_z,
            vel_z * vel_z,
        ],
        axis=1,
    )
    return jnp.einsum("ps,sfxyz->xfpyz", weights, stacked, precision=lax.Precision.HIGHEST)


def first_diff(shifted):
    return (
        0.75 * (shifted(1) - shifted(-1))
        - 0.15 * (shifted(2) - shifted(-2))
        + (shifted(3) - shifted(-3)) / 60.0
    )


def second_diff(shifted, centre):
    return (
        -49.0 / 18.0 * centre
        + 1.5 * (shifted(1) + shifted(-1))
        - 0.15 * (shifted(2) + shifted(-2))
        + (shifted(3) + shifted(-3)) / 90.0
    )


def finish_terms(owned):
    planes, bins_dev = (owned.shape[0], owned.shape[2])
    samples = owned[:, 0]
    velocity = [owned[:, 1 + comp] / samples for comp in range(3)]
    stresses = [
        owned[:, 4 + slot] / samples - velocity[pair[0]] * velocity[pair[1]]
        for slot, pair in enumerate(stress_pairs)
    ]
    fields = jnp.stack(velocity + stresses, axis=1)
    padded = padded_2(fields, (("rev", 0), ("bin", 2)), 3)

    def along(component, dim, centre):
        source = padded[:, component]
        if dim == 0:
            return lambda amount: source[3 + amount : 3 + amount + planes, 3 : 3 + bins_dev]
        if dim == 3:
            return lambda amount: source[3 : 3 + planes, 3 + amount : 3 + amount + bins_dev]
        return lambda amount: jnp.roll(centre, -amount, dim + 1)

    grad_u = [
        [first_diff(along(comp, dim, velocity[comp])) for dim in range(3)] for comp in range(3)
    ]
    unsteady, convect, produce, diffuse = ([], [], [], [])
    for slot, pair in enumerate(stress_pairs):
        first, second = pair
        stress = stresses[slot]
        unsteady.append(first_diff(along(3 + slot, 3, stress)))
        grads = [first_diff(along(3 + slot, dim, stress)) for dim in range(3)]
        convect.append(velocity[0] * grads[0] + velocity[1] * grads[1] + velocity[2] * grads[2])
        summed = jnp.zeros_like(stress)
        for dim in range(3):
            summed = (
                summed
                + stresses[pair_index(first, dim)] * grad_u[second][dim]
                + stresses[pair_index(second, dim)] * grad_u[first][dim]
            )
        produce.append(-summed)
        diffuse.append(
            viscosity
            * (
                second_diff(along(3 + slot, 0, stress), stress)
                + second_diff(along(3 + slot, 1, stress), stress)
                + second_diff(along(3 + slot, 2, stress), stress)
            )
        )
    terms_all = jnp.stack(
        [jnp.stack(unsteady), jnp.stack(convect), jnp.stack(produce), jnp.stack(diffuse)]
    )
    return (
        jnp.transpose(terms_all, (0, 1, 3, 2, 4, 5)),
        jnp.transpose(jnp.stack(velocity), (0, 2, 1, 3, 4)),
    )


def shards(snapshots, phase_index):
    frames = snapshots[0]
    bins_dev = PHASES // lax.axis_size("bin")
    local_bins = phase_index[0] - lax.axis_index("bin") * bins_dev
    exchanged = lax.all_to_all(frames, "rev", split_axis=2, concat_axis=0, tiled=True)
    all_bins = lax.all_gather(local_bins, "rev", axis=0, tiled=True)
    one_hot = (all_bins[None, :] == jnp.arange(bins_dev, dtype=jnp.int32)[:, None]).astype(
        jnp.float32
    )
    owned = binned(exchanged, one_hot)
    return finish_terms(owned)


MESH = pl.DeviceIdType.MESH
DEPTH = 2
GROUPS = 4


def turned(tile, amount, axis):
    size = tile.shape[axis]
    return pltpu.roll(tile, (-amount) % size, axis)


def both_diffs(tile, axis):
    plus = [turned(tile, s, axis) for s in (1, 2, 3)]
    minus = [turned(tile, -s, axis) for s in (1, 2, 3)]
    d1 = 0.75 * (plus[0] - minus[0]) - 0.15 * (plus[1] - minus[1]) + (plus[2] - minus[2]) * (1.0 / 60.0)
    d2 = (
        (-49.0 / 18.0) * tile
        + 1.5 * (plus[0] + minus[0])
        - 0.15 * (plus[1] + minus[1])
        + (plus[2] + minus[2]) * (1.0 / 90.0)
    )
    return d1, d2


diff_one = {1: 0.75, -1: -0.75, 2: -0.15, -2: 0.15, 3: 1.0 / 60.0, -3: -1.0 / 60.0}
diff_two = {0: -49.0 / 18.0, 1: 1.5, -1: 1.5, 2: -0.15, -2: -0.15, 3: 1.0 / 90.0, -3: 1.0 / 90.0}


def ring_weights(weights, at, size):
    row = [[] for _ in range(size)]
    for shift, weight in weights.items():
        row[(at + shift) % size].append(weight)
    return [sum(parts) for parts in row]


def weighted(row, tiles):
    total = None
    for weight, tile in zip(row, tiles):
        if weight != 0.0:
            part = weight * tile
            total = part if total is None else total + part
    return total


def moments(vel):
    return list(vel) + [vel[a] * vel[b] for a, b in stress_pairs]


def ring_kernel(
    sizes, snap, index, held, held_mean, base, late,
    own, peer, heap, fields, idx_in, idx_own, idx_peer, idx_s, tab_v, tab_s, inv_v, inv_s,
    load_sem, small_sem, idx_sem, send_sem, recv_sem, halo_send, halo_recv,
):
    snaps, nx, planes, bins, nbin = sizes
    rev, me = lax.axis_index("rev"), lax.axis_index("bin")
    left, right = lax.rem(me + nbin - 1, nbin), lax.rem(me + 1, nbin)
    other = 1 - rev

    barrier = pltpu.get_barrier_semaphore()
    for target in ((other, me), (rev, left), (rev, right)):
        pl.semaphore_signal(barrier, inc=1, device_id=target, device_id_type=MESH)
    get_index = pltpu.make_async_copy(index, idx_in, load_sem.at[1])
    get_index.start()
    whole = pltpu.make_async_copy(snap.at[0], own, load_sem.at[0])
    idx_own[...] = jnp.full(idx_own.shape, -1, jnp.int32)
    get_index.wait()
    idx_own[0:1, 0:snaps] = idx_in[...] - me * bins
    pl.semaphore_wait(barrier, 3)

    copy_idx = pltpu.make_async_remote_copy(
        src_ref=idx_own, dst_ref=idx_peer, send_sem=idx_sem.at[0], recv_sem=idx_sem.at[1],
        device_id=(other, me), device_id_type=MESH,
    )
    copy_idx.start()
    cut = snaps * 3 // 4
    pieces = [(q, 0, snaps) for q in range(nx - 1)] + [(nx - 1, 0, cut), (nx - 1, cut, snaps)]
    sends = []
    for n, (q, lo, hi) in enumerate(pieces):
        plane = lax.rem(q + planes * other, nx)
        sends.append(
            pltpu.make_async_remote_copy(
                src_ref=snap.at[0, lo:hi, :, plane], dst_ref=peer.at[q, lo:hi],
                send_sem=send_sem.at[n], recv_sem=recv_sem.at[n],
                device_id=(other, me), device_id_type=MESH,
            )
        )
    for n in range(DEPTH):
        sends[n].start()
    whole.start()

    copy_idx.wait()
    lane = lax.broadcasted_iota(jnp.int32, (1, 128), 1)
    row = jnp.where(lane < snaps, idx_own[0:1, :], pltpu.roll(idx_peer[0:1, :], snaps, 1))
    idx_own[1:2, :] = row
    to_s = pltpu.make_async_copy(idx_own, idx_s, small_sem.at[0])
    to_s.start()
    to_s.wait()

    def link(j, carry):
        prev, last, count = carry
        b = idx_s[1, j]
        prev = jnp.where((row == b) & (lane > j), j + 1, prev)
        hit = lane == b
        return prev, jnp.where(hit, j + 1, last), count + jnp.where(hit, 1.0, 0.0)

    zero_i = jnp.zeros((1, 128), jnp.int32)
    prev, last, count = lax.fori_loop(
        0, 2 * snaps, link, (zero_i, zero_i, jnp.zeros((1, 128), jnp.float32))
    )
    tab_v[...] = jnp.zeros(tab_v.shape, jnp.int32)
    tab_v[0:1, :] = prev
    tab_v[1:2, :] = last
    inv_v[...] = jnp.broadcast_to(1.0 / jnp.maximum(count, 1.0), inv_v.shape)
    to_t = pltpu.make_async_copy(tab_v, tab_s, small_sem.at[1])
    to_i = pltpu.make_async_copy(inv_v, inv_s, small_sem.at[2])
    to_t.start()
    to_i.start()
    zero = jnp.zeros(heap.shape[-2:], jnp.float32)
    for q in range(nx):
        for m in range(9):
            heap[q, 0, m] = zero
    to_t.wait()
    to_i.wait()
    whole.wait()

    def add_own(k, carry):
        before = tab_s[0, k]
        for q in range(nx):
            plane = lax.rem(q + planes * rev, nx)
            values = moments([own[k, c, plane] for c in range(3)])
            for m in range(9):
                heap[q, k + 1, m] = heap[q, before, m] + values[m]
        return carry

    lax.fori_loop(0, snaps, add_own, 0)

    def add_peer(q, lo, hi):
        def body(k, carry):
            before = tab_s[0, k + snaps]
            values = moments([peer[q, k, c] for c in range(3)])
            for m in range(9):
                heap[q, k + snaps + 1, m] = heap[q, before, m] + values[m]
            return carry

        lax.fori_loop(lo, hi, body, 0)

    def finish(q):
        def body(p, carry):
            at = tab_s[1, p]
            scale = inv_s[0, p]
            vel = [heap[q, at, c] * scale for c in range(3)]
            stress = [
                heap[q, at, 3 + m] * scale - vel[a] * vel[b] for m, (a, b) in enumerate(stress_pairs)
            ]
            if q == nx - 1:
                for n, tile in enumerate(vel + stress):
                    late[p, n] = tile
            else:
                for n, tile in enumerate(vel + stress):
                    fields[q, n, p + 3] = tile
            if q < planes:
                for c in range(3):
                    held_mean[c, p, q] = vel[c]
                    base[p, c, q] = stress[pair_index(c, 0)]
            return carry

        lax.fori_loop(0, bins, body, 0)

    def in_plane(q):
        def body(p, carry):
            vel = [fields[q, c, p + 3] for c in range(3)]
            stress = [fields[q, 3 + m, p + 3] for m in range(6)]
            grad = []
            for c in range(3):
                grad.append([both_diffs(vel[c], 0)[0], both_diffs(vel[c], 1)[0]])
            for m, (a, b) in enumerate(stress_pairs):
                y1, y2 = both_diffs(stress[m], 0)
                z1, z2 = both_diffs(stress[m], 1)
                held[1, m, p, q] = vel[1] * y1 + vel[2] * z1
                held[3, m, p, q] = y2 + z2
                total = None
                for k in (1, 2):
                    part = stress[pair_index(a, k)] * grad[b][k - 1] + stress[pair_index(b, k)] * grad[a][k - 1]
                    total = part if total is None else total + part
                held[2, m, p, q] = total
            return carry

        lax.fori_loop(0, bins, body, 0)

    halos = []
    for q in range(planes):
        halos.append(
            (
                pltpu.make_async_remote_copy(
                    src_ref=fields.at[q, 3:9, 3:6], dst_ref=fields.at[q, 3:9, bins + 3 : bins + 6],
                    send_sem=halo_send.at[2 * q], recv_sem=halo_recv.at[2 * q],
                    device_id=(rev, left), device_id_type=MESH,
                ),
                pltpu.make_async_remote_copy(
                    src_ref=fields.at[q, 3:9, bins : bins + 3], dst_ref=fields.at[q, 3:9, 0:3],
                    send_sem=halo_send.at[2 * q + 1], recv_sem=halo_recv.at[2 * q + 1],
                    device_id=(rev, right), device_id_type=MESH,
                ),
            )
        )

    def in_phase(q):
        def body(p, carry):
            for m in range(6):
                f = lambda s: fields[q, 3 + m, p + 3 + s]
                held[0, m, p, q] = (
                    0.75 * (f(1) - f(-1)) - 0.15 * (f(2) - f(-2)) + (f(3) - f(-3)) * (1.0 / 60.0)
                )
            return carry

        lax.fori_loop(0, bins, body, 0)

    one = [ring_weights(diff_one, q, nx)[: nx - 1] for q in range(planes)]
    two = [ring_weights(diff_two, q, nx)[: nx - 1] for q in range(planes)]

    def across(p, carry):
        grad = []
        for c in range(3):
            tiles = [fields[q, c, p + 3] for q in range(nx - 1)]
            grad.append([weighted(one[q], tiles) for q in range(planes)])
        for m, (a, b) in enumerate(stress_pairs):
            tiles = [fields[q, 3 + m, p + 3] for q in range(nx - 1)]
            for q in range(planes):
                held[1, m, p, q] = held[1, m, p, q] + fields[q, 0, p + 3] * weighted(one[q], tiles)
                held[3, m, p, q] = viscosity * (held[3, m, p, q] + weighted(two[q], tiles))
                part = (
                    fields[q, 3 + pair_index(a, 0), p + 3] * grad[b][q]
                    + fields[q, 3 + pair_index(b, 0), p + 3] * grad[a][q]
                )
                held[2, m, p, q] = -(held[2, m, p, q] + part)
        return carry

    for n, (q, lo, hi) in enumerate(pieces):
        sends[n].wait()
        if n + DEPTH < len(pieces):
            sends[n + DEPTH].start()
        add_peer(q, lo, hi)
        if hi == snaps:
            finish(q)
        if q < planes:
            for halo in halos[q]:
                halo.start()
            in_plane(q)
        if 1 <= q <= planes:
            for halo in halos[q - 1]:
                halo.wait()
            in_phase(q - 1)
        if q == nx - 2:
            lax.fori_loop(0, bins, across, 0)


def last_kernel(sizes, held, held_mean, base, late, terms, mean, done, out_sem):
    nx, planes, bins = sizes
    outs = [
        pltpu.make_async_copy(held.at[0], terms.at[0], out_sem.at[0]),
        pltpu.make_async_copy(held_mean, mean, out_sem.at[1]),
    ]
    for out in outs:
        out.start()
    one = [ring_weights(diff_one, q, nx)[nx - 1] for q in range(planes)]
    two = [viscosity * ring_weights(diff_two, q, nx)[nx - 1] for q in range(planes)]

    def body(p, carry):
        vel = [late[p, c] for c in range(3)]
        stress = [late[p, 3 + m] for m in range(6)]
        for q in range(planes):
            vel_x = held_mean[0, p, q] * one[q]
            near = [base[p, c, q] * one[q] for c in range(3)]
            for m, (a, b) in enumerate(stress_pairs):
                done[0, m, p, q] = held[1, m, p, q] + vel_x * stress[m]
                done[1, m, p, q] = held[2, m, p, q] - (near[a] * vel[b] + near[b] * vel[a])
                done[2, m, p, q] = held[3, m, p, q] + two[q] * stress[m]
        return carry

    each = bins // GROUPS
    for g in range(GROUPS):
        lax.fori_loop(g * each, (g + 1) * each, body, 0)
        out = pltpu.make_async_copy(
            done.at[:, :, g * each : (g + 1) * each],
            terms.at[1:4, :, g * each : (g + 1) * each],
            out_sem.at[2 + g],
        )
        out.start()
        outs.append(out)
    for out in outs:
        out.wait()


def paired_shards(snapshots, phase_index):
    _, snaps, _, nx, ny, nz = snapshots.shape
    nbin, nrev = lax.axis_size("bin"), lax.axis_size("rev")
    bins, planes = PHASES // nbin, nx // nrev
    f32, i32 = jnp.float32, jnp.int32
    vmem, dma = pltpu.VMEM, pltpu.SemaphoreType.DMA
    anywhere = pl.BlockSpec(memory_space=pl.ANY)
    near = pl.BlockSpec(memory_space=pltpu.VMEM)
    snapshots = pltpu.with_memory_space_constraint(snapshots, pltpu.HBM)
    phase_index = pltpu.with_memory_space_constraint(phase_index, pltpu.HBM)
    parts = pl.pallas_call(
        functools.partial(ring_kernel, (snaps, nx, planes, bins, nbin)),
        out_shape=(
            vmem((4, 6, bins, planes, ny, nz), f32),
            vmem((3, bins, planes, ny, nz), f32),
            vmem((bins, 3, planes, ny, nz), f32),
            vmem((bins, 9, ny, nz), f32),
        ),
        in_specs=[pl.BlockSpec(memory_space=pltpu.HBM)] * 2,
        out_specs=[near] * 4,
        scratch_shapes=[
            vmem((snaps, 3, nx, ny, nz), f32),
            vmem((nx, snaps, 3, ny, nz), f32),
            vmem((nx, 2 * snaps + 1, 9, ny, nz), f32),
            vmem((nx - 1, 9, bins + 6, ny, nz), f32),
            vmem((1, snaps), i32),
            vmem((8, 128), i32),
            vmem((8, 128), i32),
            pltpu.SMEM((8, 128), i32),
            vmem((8, 128), i32),
            pltpu.SMEM((8, 128), i32),
            vmem((8, 128), f32),
            pltpu.SMEM((8, 128), f32),
            dma((2,)),
            dma((3,)),
            dma((2,)),
            dma((nx + 1,)),
            dma((nx + 1,)),
            dma((2 * planes,)),
            dma((2 * planes,)),
        ],
        compiler_params=pltpu.CompilerParams(
            collective_id=0, has_side_effects=True, vmem_limit_bytes=40 * 1024 * 1024
        ),
        cost_estimate=pl.CostEstimate(flops=60_000_000, bytes_accessed=8_000_000, transcendentals=0),
    )(snapshots, phase_index)
    parts = [pltpu.with_memory_space_constraint(part, pltpu.VMEM) for part in parts]
    return pl.pallas_call(
        functools.partial(last_kernel, (nx, planes, bins)),
        out_shape=(
            jax.ShapeDtypeStruct((4, 6, bins, planes, ny, nz), f32),
            jax.ShapeDtypeStruct((3, bins, planes, ny, nz), f32),
        ),
        in_specs=[near] * 4,
        out_specs=[anywhere] * 2,
        scratch_shapes=[vmem((3, 6, bins, planes, ny, nz), f32), dma((2 + GROUPS,))],
        compiler_params=pltpu.CompilerParams(vmem_limit_bytes=16 * 1024 * 1024),
        cost_estimate=pl.CostEstimate(flops=4_000_000, bytes_accessed=8_000_000, transcendentals=0),
    )(*parts)


def fits_pairs(mesh, snapshots):
    nrev, nbin = mesh.shape["rev"], mesh.shape["bin"]
    snaps, planes, bins = snapshots.shape[1] // nbin, snapshots.shape[3] // nrev, PHASES // nbin
    whole_tiles = snapshots.shape[4:] == (8, 128)
    return nrev == 2 and nbin >= 3 and planes == 3 and 2 * snaps <= 128 and bins % GROUPS == 0 and bins <= 128 and whole_tiles


def solution(mesh):
    in_specs = (P("rev", "bin", None, None, None, None), P("rev", "bin"))
    out_specs = (P(None, None, "bin", "rev", None, None), P(None, "bin", "rev", None, None))

    def run(snapshots, phase_index):
        body = paired_shards if fits_pairs(mesh, snapshots) else shards
        mapped = jax.shard_map(body, mesh=mesh, in_specs=in_specs, out_specs=out_specs, check_vma=False)
        return mapped(snapshots, phase_index)

    return run
```

profile of v0, /device:TPU:0, one launch (start us, length us, event | category | flops | bytes accessed | tf_op | source)
XLA Modules:
  0.0 60.0 jit_solution(15109285286769705378)
XLA Ops:
  0.6 56.9 %shard_map.41 = (f32[4,6,16,3,8,128]{5,4,3,2,1,0:T(8,128)S(1)}, f32[3,16,3,8,128]{4,3,2,1,0:T(8,128)S(1)}, f32[16,3,3,8,128]{4,3,2,1,0:T(8,128)S(1)}, f32[16,9,8,128]{3,2,1,0:T(8,128)S(1)}) custom-call(f32[1,32,3,6,8,128]{5,4,3,2,1,0:T(8,128)} %snap.1, s32[1,32]{1,0:T(1,128)} %index.1), custom_call_target="tpu_custom_call" | custom-call | flops 60000000 | bytes 8000000 | tf_op jit(solution)/shard_map/pallas_call | solution.py:444
  57.6 2.4 %shard_map.42 = (f32[4,6,16,3,8,128]{5,4,3,2,1,0:T(8,128)}, f32[3,16,3,8,128]{4,3,2,1,0:T(8,128)}) custom-call(f32[4,6,16,3,8,128]{5,4,3,2,1,0:T(8,128)S(1)} %get-tuple-element.6.held, f32[3,16,3,8,128]{4,3,2,1,0:T(8,128)S(1)} %get-tuple-element.7.held_mean, f32[16,3,3,8,128]{4,3,2,1,0:T(8,128)S(1)} %get-tuple-element.8.base, ...), custom_call_target="tpu_custom_call" | custom-call | flops 4000000 | bytes 8000000 | tf_op jit(solution)/shard_map/pallas_call | solution.py:481
where the time goes:
time: 60.1 us; the launch traced here: 60 us
  Pallas kernels  59.4 us (99%)
  between operations  0.64 us (1%)
    pallas_call x1, Pallas kernels, paired_shards(): pl.pallas_call(functools.partial(ring_kernel, (snaps, nx, planes, bins, n...  56.9 us
    pallas_call x1, Pallas kernels, paired_shards(): pl.pallas_call(functools.partial(last_kernel, (nx, planes, bins)), out_sh...  2.42 us

commit v1 on v0

--- a/solution.py
+++ b/solution.py
@@ -141,7 +141,8 @@
 
 MESH = pl.DeviceIdType.MESH
 DEPTH = 2
-GROUPS = 4
+GROUPS = 8
+PIECES = 4
 
 
 def turned(tile, amount, axis):
@@ -212,8 +213,9 @@
         device_id=(other, me), device_id_type=MESH,
     )
     copy_idx.start()
-    cut = snaps * 3 // 4
-    pieces = [(q, 0, snaps) for q in range(nx - 1)] + [(nx - 1, 0, cut), (nx - 1, cut, snaps)]
+    cut = snaps // PIECES
+    pieces = [(q, 0, snaps) for q in range(nx - 1)]
+    pieces += [(nx - 1, n * cut, (n + 1) * cut) for n in range(PIECES)]
     sends = []
     for n, (q, lo, hi) in enumerate(pieces):
         plane = lax.rem(q + planes * other, nx)
@@ -282,7 +284,7 @@
                 heap[q, k + snaps + 1, m] = heap[q, before, m] + values[m]
             return carry
 
-        lax.fori_loop(lo, hi, body, 0)
+        lax.fori_loop(lo, hi, body, 0, unroll=4)
 
     def finish(q):
         def body(p, carry):
@@ -304,7 +306,7 @@
                     base[p, c, q] = stress[pair_index(c, 0)]
             return carry
 
-        lax.fori_loop(0, bins, body, 0)
+        lax.fori_loop(0, bins, body, 0, unroll=4)
 
     def in_plane(q):
         def body(p, carry):
@@ -419,7 +421,7 @@
 
     each = bins // GROUPS
     for g in range(GROUPS):
-        lax.fori_loop(g * each, (g + 1) * each, body, 0)
+        lax.fori_loop(g * each, (g + 1) * each, body, 0, unroll=True)
         out = pltpu.make_async_copy(
             done.at[:, :, g * each : (g + 1) * each],
             terms.at[1:4, :, g * each : (g + 1) * each],
@@ -467,8 +469,8 @@
             dma((2,)),
             dma((3,)),
             dma((2,)),
-            dma((nx + 1,)),
-            dma((nx + 1,)),
+            dma((nx - 1 + PIECES,)),
+            dma((nx - 1 + PIECES,)),
             dma((2 * planes,)),
             dma((2 * planes,)),
         ],
@@ -496,7 +498,7 @@
     nrev, nbin = mesh.shape["rev"], mesh.shape["bin"]
     snaps, planes, bins = snapshots.shape[1] // nbin, snapshots.shape[3] // nrev, PHASES // nbin
     whole_tiles = snapshots.shape[4:] == (8, 128)
-    return nrev == 2 and nbin >= 3 and planes == 3 and 2 * snaps <= 128 and bins % GROUPS == 0 and bins <= 128 and whole_tiles
+    return nrev == 2 and nbin >= 3 and planes == 3 and 2 * snaps <= 128 and bins % GROUPS == 0 and snaps % (4 * PIECES) == 0 and bins <= 128 and whole_tiles
 
 
 def solution(mesh):

time: 60.1 us -> 62.4 us (1.038)
  Pallas kernels: 59.4 us -> 61.6 us
    pallas_call x1, Pallas kernels: 56.9 us -> 59.1 us  [paired_shards(): pl.pallas_call(functools.partial(ring_kernel, (snaps, nx, planes, bins, n...]
where the time goes in v1:
time: 62.4 us; the launch traced here: 62.2 us
  Pallas kernels  61.6 us (99%)
  between operations  0.64 us (1%)
    pallas_call x1, Pallas kernels, paired_shards(): pl.pallas_call(functools.partial(ring_kernel, (snaps, nx, planes, bins, n...  59.1 us
    pallas_call x1, Pallas kernels, paired_shards(): pl.pallas_call(functools.partial(last_kernel, (nx, planes, bins)), out_sh...  2.44 us

profile of v1, /device:TPU:0, one launch (start us, length us, event | category | flops | bytes accessed | tf_op | source)
XLA Modules:
  0.0 62.2 jit_solution(4093735722561905231)
XLA Ops:
  0.6 59.1 %shard_map.41 = (f32[4,6,16,3,8,128]{5,4,3,2,1,0:T(8,128)S(1)}, f32[3,16,3,8,128]{4,3,2,1,0:T(8,128)S(1)}, f32[16,3,3,8,128]{4,3,2,1,0:T(8,128)S(1)}, f32[16,9,8,128]{3,2,1,0:T(8,128)S(1)}) custom-call(f32[1,32,3,6,8,128]{5,4,3,2,1,0:T(8,128)} %snap.1, s32[1,32]{1,0:T(1,128)} %index.1), custom_call_target="tpu_custom_call" | custom-call | flops 60000000 | bytes 8000000 | tf_op jit(solution)/shard_map/pallas_call | solution.py:446
  59.8 2.4 %shard_map.42 = (f32[4,6,16,3,8,128]{5,4,3,2,1,0:T(8,128)}, f32[3,16,3,8,128]{4,3,2,1,0:T(8,128)}) custom-call(f32[4,6,16,3,8,128]{5,4,3,2,1,0:T(8,128)S(1)} %get-tuple-element.6.held, f32[3,16,3,8,128]{4,3,2,1,0:T(8,128)S(1)} %get-tuple-element.7.held_mean, f32[16,3,3,8,128]{4,3,2,1,0:T(8,128)S(1)} %get-tuple-element.8.base, ...), custom_call_target="tpu_custom_call" | custom-call | flops 4000000 | bytes 8000000 | tf_op jit(solution)/shard_map/pallas_call | solution.py:483
